TPU v7x, 512 devices: a whole 4x8x8 slice. The times are simulated.
512 devices in a mesh: mem: 32 (over z, x), geo: 16 (over y, core).
Axes of the slice: x: 4, y: 8, z: 8, core: 2. Of those that a mesh axis runs over, the one named last changes fastest.
Arguments:
- control: float32 [32, 32, 48, 384], P('mem', 'geo'), may hold values from -6 to 6
- kappa_table: float32 [16], replicated, may hold values from 0.02 to 0.24
- kappa_index: int32 [48, 384], replicated, may hold values from 0 to 15
- tile_bounds: int32 [17], replicated, may hold values from 0 to 18432, as said below
- filter_bands: float32 [16, 5, 32], replicated, may hold values from -0.3 to 0.3
- perturbation: bfloat16 [2, 32, 32, 18432], P(None, 'mem', None, 'geo'), may hold values from -6 to 6
Outputs:
- increment: float32 [2, 32, 18432], P(None, 'mem', 'geo')
Inputs may be any that keep to these rules, and one draw needn't show every extreme that they name: tile_bounds[0] is 0, tile_bounds[16] is 18432, and the bounds never fall; tile t holds columns tile_bounds[t] to tile_bounds[t + 1] - 1.
All inputs are finite; a program needn't handle non-finite values.
Results may differ from a plain program's by a relative error of at most 0.005.
Values may be sent and summed in bfloat16 or wider, within the bound.
No kernel may reach another device: no remote copies, remote signals or barrier semaphores. Data moves between devices by JAX's collectives and lax.ppermute only.
A program may use at most 64 MiB of HBM per device.

v0:
```python
import jax
import jax.numpy as jnp
from jax import lax
from jax.sharding import PartitionSpec as P

ITERS = 10


def neighbours(state):
    east = jnp.concatenate([state[..., 1:, :], state[..., -1:, :]], axis=-2)
    west = jnp.concatenate([state[..., :1, :], state[..., :-1, :]], axis=-2)
    north = jnp.concatenate([state[..., 1:], state[..., -1:]], axis=-1)
    south = jnp.concatenate([state[..., :1], state[..., :-1]], axis=-1)
    return (east, west, north, south)


def face_weights(kappa_field):
    return tuple((0.5 * (kappa_field + other) for other in neighbours(kappa_field)))


def diffuse_step(state, weights):
    east, west, north, south = neighbours(state)
    update = weights[0] * (east - state) + weights[1] * (west - state)
    update = update + weights[2] * (north - state) + weights[3] * (south - state)
    return state + update


def vertical_filter(values, coefficients):
    levels = values.shape[0]
    padded = jnp.pad(values, ((2, 2), (0, 0)))
    result = values
    for offset in range(5):
        result = result + coefficients[offset] * padded[offset : offset + levels]
    return result


def body(control, kappa_table, kappa_index, tile_bounds, filter_bands, perturbation):
    kappa_field = jnp.zeros(kappa_index.shape, jnp.float32)
    for entry in range(kappa_table.shape[0]):
        kappa_field = kappa_field + jnp.where(kappa_index == entry, kappa_table[entry], 0.0)
    weights = face_weights(kappa_field)
    state_field = lax.fori_loop(0, ITERS, lambda step, cur: diffuse_step(cur, weights), control)
    flattened = state_field.reshape(state_field.shape[0], state_field.shape[1], -1)
    by_columns = lax.all_to_all(flattened, "geo", split_axis=2, concat_axis=1, tiled=True)
    width = by_columns.shape[2]
    tiles_count = filter_bands.shape[0]
    columns = lax.axis_index("geo") * width + jnp.arange(width, dtype=jnp.int32)
    tile_ids = jnp.sum((columns[None, :] >= tile_bounds[1:-1][:, None]).astype(jnp.int32), axis=0)
    one_hot = (tile_ids[None, :] == jnp.arange(tiles_count, dtype=jnp.int32)[:, None]).astype(
        jnp.float32
    )
    coefficients = jnp.einsum("tkl,tc->klc", filter_bands, one_hot, precision=lax.Precision.HIGHEST)
    filtered = vertical_filter(by_columns[0], coefficients).astype(jnp.bfloat16)
    products = perturbation[:, 0].astype(jnp.float32) * filtered.astype(jnp.float32)[None]
    return lax.psum_scatter(products, "mem", scatter_dimension=1, tiled=True)


def solution(mesh):
    in_specs = (P("mem", "geo", None, None), P(), P(), P(), P(), P(None, "mem", None, "geo"))
    out_specs = P(None, "mem", "geo")
    return jax.shard_map(body, mesh=mesh, in_specs=in_specs, out_specs=out_specs, check_vma=False)
```

profile of v0, /device:TPU:8, one launch (start us, length us, event | category | flops | bytes accessed | tf_op | source)
XLA Modules:
  0.0 340.9 jit_solution(5433511955447139947)
XLA Ops:
  6.5 0.0 copy-start
  6.5 0.9 copy.26
  7.5 1.9 fusion.35
  9.4 10.9 %select_add_fusion = f32[48,384]{1,0:T(8,128)S(1)} fusion(s32[48,384]{1,0:T(8,128)} %param.10, f32[]{:T(128)} %bitcast.16, f32[]{:T(128)} %bitcast.15, f32[]{:T(128)} %bitcast.14, f32[]{:T(128)} %bitcast.13, f32[]{:T(128)} %bitcast.12, f32[]{:T(128)} %bitcast.11, f32[]{:T(128)} %bitcast.10, f32[]{:T(128)} %bitcast.9, f32[]{:T(128)} %bitcast.8, f32[]{:T(128)} %bitcast.7, ...), kind=kLoop, calls=%fused_computation.44 | loop fusion | flops 866304 | bytes 147520 | tf_op jit(solution)/shard_map/add | solution.py:40
  20.3 0.1 fusion.32
  20.4 0.1 fusion.31
  20.5 11.0 %fusion.22 = (f32[48,384]{1,0:T(8,128)S(1)}, f32[48,384]{1,0:T(8,128)S(1)}, f32[48,384]{1,0:T(8,128)S(1)}, f32[48,384]{1,0:T(8,128)S(1)}) fusion(f32[48,383]{1,0:T(8,128)S(1)} %get-tuple-element.64, f32[48,1]{1,0:T(8,128)S(1)} %get-tuple-element.62, f32[48,1]{1,0:T(8,128)S(1)} %get-tuple-element.63, f32[48,383]{1,0:T(8,128)S(1)} %get-tuple-element.65, ...), kind=kLoop, calls=%fused_computation.41 | loop fusion | flops 1087488 | bytes 663616 | tf_op jit(solution)/shard_map/mul | solution.py:18
  31.5 4.1 %while.10 = (s32[]{:T(128)}, f32[1,2,48,384]{3,2,1,0:T(8,128)S(1)}, f32[48,384]{1,0:T(8,128)S(1)}, f32[48,384]{1,0:T(8,128)S(1)}, f32[48,384]{1,0:T(8,128)S(1)}, /*index=5*/f32[48,384]{1,0:T(8,128)S(1)}, s32[]{:T(128)}) while((s32[]{:T(128)}, f32[1,2,48,384]{3,2,1,0:T(8,128)S(1)}, f32[48,384]{1,0:T(8,128)S(1)}, f32[48,384]{1,0:T(8,128)S(1)}, ...), condition=%wide.region_1.2_spmd, body=%wide.region_0.1_spmd.sunk | while | flops 589826 | bytes 2359373 | solution.py:42
  31.5 0.1 fusion.45
  31.6 0.1 fusion.44
  31.7 0.2 fusion.46
  31.9 0.1 fusion.45
  32.0 0.1 fusion.44
  32.1 0.2 fusion.46
  32.3 0.1 fusion.45
  32.4 0.1 fusion.44
  32.5 0.2 fusion.46
  32.7 0.1 fusion.45
  32.9 0.1 fusion.44
  32.9 0.2 fusion.46
  33.2 0.1 fusion.45
  33.3 0.1 fusion.44
  33.4 0.2 fusion.46
  33.6 0.1 fusion.45
  33.7 0.1 fusion.44
  33.8 0.2 fusion.46
  34.0 0.1 fusion.45
  34.1 0.1 fusion.44
  34.2 0.2 fusion.46
  34.4 0.1 fusion.45
  34.5 0.1 fusion.44
  34.6 0.2 fusion.46
  34.8 0.1 fusion.45
  34.9 0.1 fusion.44
  35.0 0.2 fusion.46
  35.2 0.1 fusion.45
  35.3 0.1 fusion.44
  35.4 0.2 fusion.46
  35.6 5.6 %copy.13 = f32[1,2,48,384]{1,3,2,0:T(8,128)} copy(f32[1,2,48,384]{3,2,1,0:T(8,128)S(1)} %get-tuple-element.37) | data formatting | bytes 294912 | tf_op jit(solution)/shard_map/while | solution.py:42
  41.2 0.5 broadcast.25
  41.7 83.6 %reduce = f32[18432,2]{1,0:T(8,128)} reduce(f32[18432,1,2]{2,1,0:T(1,128)} %bitcast.63, f32[]{:T(128)} %broadcast.25), dimensions={1}, to_apply=%bitcast.60.reduce_sub_computation | reduce | bytes 294916
  125.2 0.0 copy-start.2
  125.3 8.9 %reshape.29 = f32[16,1,2304]{2,1,0:T(1,128)} reshape(f32[18432,2]{1,0:T(8,128)} %reduce) | data formatting | bytes 294912
  134.1 9.1 %all-to-all-start = ((f32[16,1,2304]{2,1,0:T(1,128)}), f32[16,1,2304]{2,1,0:T(1,128)S(1)}, u32[]{:S(2)}, u32[]{:S(2)}) async-start(f32[16,1,2304]{2,1,0:T(1,128)} %reshape.29), calls=%async_computation | async-start | bytes 294912 | tf_op jit(solution)/shard_map/all_to_all | solution.py:44
  143.3 0.2 all-reduce.4.cloned.1.call-start
  143.5 0.0 copy-done.2
  143.5 0.1 slice.151
  143.6 0.1 convert_reduce_fusion
  143.7 0.0 copy-done
  143.7 0.5 convolution_bitcast_fusion
  144.2 6.8 %all-to-all-done = f32[16,1,2304]{2,1,0:T(1,128)S(1)} async-done(((f32[16,1,2304]{2,1,0:T(1,128)}), f32[16,1,2304]{2,1,0:T(1,128)S(1)}, u32[]{:S(2)}, u32[]{:S(2)}) %all-to-all-start) | async-done | bytes 147488 | tf_op jit(solution)/shard_map/all_to_all | solution.py:44
  151.0 1.0 reduce.1
  152.0 0.0 copy-start.1
  152.0 17.8 %reshape.30 = f32[18432,1,2]{2,1,0:T(1,128)} reshape(f32[16,2304]{1,0:T(8,128)S(1)} %reduce.1) | data formatting | bytes 294912
  169.9 5.6 %copy.14 = f32[1,2,16,1152]{3,1,2,0:T(2,128)S(1)} copy(f32[1,2,16,1152]{1,3,2,0:T(8,128)} %bitcast.64) | data formatting | bytes 294912 | tf_op jit(solution)/shard_map/all_to_all | solution.py:44
  175.5 0.1 squeeze.83
  175.6 0.1 fusion.25
  175.7 0.0 copy-done.1
  175.7 0.9 convert_multiply_fusion
  176.6 0.0 all-reduce.4.cloned.1.call-update
  176.6 1.3 dynamic-slice
  177.9 154.2 %all-reduce.4.cloned.1.call-done = f32[2,32,1152]{2,0,1:T(2,128)} async-done(((f32[2,32,1152]{2,0,1:T(2,128)}), f32[2,32,1152]{2,0,1:T(2,128)}) %all-reduce.4.cloned.1.call-update) | async-done | bytes 294928
  332.1 1.3 constant_dynamic-slice_fusion
  333.4 0.6 copy.15
  (23 shorter events, 0.3 us)
Async XLA Ops:
  6.5 137.2 %copy-start = (f32[16,5,32]{2,0,1:T(8,128)S(1)}, f32[16,5,32]{2,0,1:T(8,128)}, u32[]{:S(2)}) copy-start(f32[16,5,32]{2,0,1:T(8,128)} %param.12) | copy-start | bytes 30724
  125.2 18.3 %copy-start.2 = (s32[17]{0:T(128)S(1)}, s32[17]{0:T(128)}, u32[]{:S(2)}) copy-start(s32[17]{0:T(128)} %param.11) | copy-start | bytes 208
  134.1 16.9 %all-to-all-start = ((f32[16,1,2304]{2,1,0:T(1,128)}), f32[16,1,2304]{2,1,0:T(1,128)S(1)}, u32[]{:S(2)}, u32[]{:S(2)}) async-start(f32[16,1,2304]{2,1,0:T(1,128)} %reshape.29), calls=%async_computation | async-start | bytes 294912 | tf_op jit(solution)/shard_map/all_to_all | solution.py:44
  143.3 188.8 %all-reduce.4.cloned.1.call-start = ((), (), s32[]{:S(2)}) async-start(), calls=%async_computation.1 | async-start | bytes 589824
  152.0 23.7 %copy-start.1 = (bf16[2,1,32,1152]{3,2,1,0:T(8,128)(2,1)S(1)}, bf16[2,1,32,1152]{3,2,1,0:T(8,128)(2,1)}, u32[]{:S(2)}) copy-start(bf16[2,1,32,1152]{3,2,1,0:T(8,128)(2,1)} %param.13) | copy-start | bytes 442372
Sparse Core Ops, SparseCore 0:
  176.7 155.3 all-reduce.3
where the time goes:
time: 342 us; the launch traced here: 341 us
  waiting for transfers between devices  161 us (47%)
  other arithmetic  109 us (32%)
  local copies, waits for them, and re-layouts  47 us (14%)
  between operations  13.5 us (4%)
  starting transfers between devices  9.35 us (3%)
    unnamed x2, waiting for transfers between devices  154 us
    unnamed x1, other arithmetic  83.6 us
    unnamed x12, local copies, waits for them, and re-layouts  30.8 us
    mul x1, other arithmetic, face_weights(): 0.5 * (kappa_field + other)  11 us
    add x1, other arithmetic, body(): kappa_field + jnp.where(kappa_index == entry, kappa_table[entry], 0.0)  10.9 us
    all_to_all x1, starting transfers between devices, body(): lax.all_to_all(flattened, 'geo', split_axis=2, concat_axis=1, tiled=True)  9.13 us
  transfers between devices with their start and end apart: 2, of which 2 were waited for; matrix products, arithmetic and copies ran while one was open for 1% of the time, Pallas kernels for 0%

commit v1 on v0

--- a/solution.py
+++ b/solution.py
@@ -41,7 +41,10 @@
     weights = face_weights(kappa_field)
     state_field = lax.fori_loop(0, ITERS, lambda step, cur: diffuse_step(cur, weights), control)
     flattened = state_field.reshape(state_field.shape[0], state_field.shape[1], -1)
-    by_columns = lax.all_to_all(flattened, "geo", split_axis=2, concat_axis=1, tiled=True)
+    by_columns = jnp.concatenate(
+        lax.all_to_all(jnp.stack(jnp.split(flattened, lax.axis_size("geo"), axis=2)), "geo", 0, 0),
+        axis=1,
+    )
     width = by_columns.shape[2]
     tiles_count = filter_bands.shape[0]
     columns = lax.axis_index("geo") * width + jnp.arange(width, dtype=jnp.int32)

time: 342 us -> 226 us (0.66)
  other arithmetic: 109 us -> 23.2 us
  local copies, waits for them, and re-layouts: 47 us -> 18.2 us
    unnamed x1 -> x0, other arithmetic: 83.6 us -> none
    unnamed x12 -> x29, local copies, waits for them, and re-layouts: 30.8 us -> 13.8 us
    while x1 -> x0, local copies, waits for them, and re-layouts: 5.61 us -> none  [body(): lax.fori_loop(0, ITERS, lambda step, cur: diffuse_step(cur, weights), con...]
    all_to_all x1 -> x0, local copies, waits for them, and re-layouts: 5.6 us -> none  [body(): lax.all_to_all(flattened, 'geo', split_axis=2, concat_axis=1, tiled=True)]
where the time goes in v1:
time: 226 us
  waiting for transfers between devices  161 us (71%)
  other arithmetic  23.2 us (10%)
  local copies, waits for them, and re-layouts  18.2 us (8%)
  between operations  13.5 us (6%)
  starting transfers between devices  9.17 us (4%)
    unnamed x2, waiting for transfers between devices  154 us
    unnamed x29, local copies, waits for them, and re-layouts  13.8 us
    mul x1, other arithmetic, face_weights(): 0.5 * (kappa_field + other)  10.3 us
    add x1, other arithmetic, body(): kappa_field + jnp.where(kappa_index == entry, kappa_table[entry], 0.0)  10.3 us
    all_to_all x1, starting transfers between devices, body(): lax.all_to_all(jnp.stack(jnp.split(flattened, lax.axis_size('geo'), axis=...  9.13 us
    all_to_all x1, waiting for transfers between devices, body(): lax.all_to_all(jnp.stack(jnp.split(flattened, lax.axis_size('geo'), axis=...  6.35 us
  transfers between devices with their start and end apart: 2, of which 2 were waited for; matrix products, arithmetic and copies ran while one was open for 1% of the time, Pallas kernels for 0%

profile of v1, /device:TPU:8, one launch (start us, length us, event | category | flops | bytes accessed | tf_op | source)
XLA Modules:
  0.0 225.7 jit_solution(3990329394365274593)
XLA Ops:
  6.5 0.7 copy-done.4
  7.2 0.7 fusion.35
  7.9 0.2 copy-done.2
  8.1 10.3 %select_add_fusion = f32[48,384]{1,0:T(8,128)S(1)} fusion(s32[48,384]{1,0:T(8,128)S(1)} %copy-done.2, f32[]{:T(128)} %bitcast.16, f32[]{:T(128)} %bitcast.15, f32[]{:T(128)} %bitcast.14, f32[]{:T(128)} %bitcast.13, f32[]{:T(128)} %bitcast.12, f32[]{:T(128)} %bitcast.11, f32[]{:T(128)} %bitcast.10, f32[]{:T(128)} %bitcast.9, f32[]{:T(128)} %bitcast.8, ...), kind=kLoop, calls=%fused_computation.44 | loop fusion | flops 866304 | bytes 147520 | tf_op jit(solution)/shard_map/add | solution.py:40
  18.4 0.1 fusion.32
  18.6 10.3 %fusion.22 = (f32[48,384]{1,0:T(8,128)S(1)}, f32[48,384]{1,0:T(8,128)S(1)}, f32[48,384]{1,0:T(8,128)S(1)}, f32[48,384]{1,0:T(8,128)S(1)}) fusion(f32[48,383]{1,0:T(8,128)S(1)} %get-tuple-element.64, f32[48,1]{1,0:T(8,128)S(1)} %get-tuple-element.62, f32[48,1]{1,0:T(8,128)S(1)} %get-tuple-element.63, f32[48,383]{1,0:T(8,128)S(1)} %get-tuple-element.65, ...), kind=kLoop, calls=%fused_computation.41 | loop fusion | flops 1087488 | bytes 663616 | tf_op jit(solution)/shard_map/mul | solution.py:18
  28.9 4.0 %while.10 = (s32[]{:T(128)}, f32[1,2,48,384]{3,2,1,0:T(8,128)S(1)}, f32[48,384]{1,0:T(8,128)S(1)}, f32[48,384]{1,0:T(8,128)S(1)}, f32[48,384]{1,0:T(8,128)S(1)}, /*index=5*/f32[48,384]{1,0:T(8,128)S(1)}, s32[]{:T(128)}) while((s32[]{:T(128)}, f32[1,2,48,384]{3,2,1,0:T(8,128)S(1)}, f32[48,384]{1,0:T(8,128)S(1)}, f32[48,384]{1,0:T(8,128)S(1)}, ...), condition=%wide.region_1.2_spmd, body=%wide.region_0.1_spmd.sunk | while | flops 589826 | bytes 2359373 | solution.py:42
  29.0 0.1 fusion.45
  29.1 0.1 fusion.44
  29.2 0.2 fusion.46
  29.4 0.1 fusion.45
  29.5 0.1 fusion.44
  29.6 0.2 fusion.46
  29.8 0.1 fusion.45
  29.9 0.1 fusion.44
  30.0 0.2 fusion.46
  30.2 0.1 fusion.45
  30.3 0.1 fusion.44
  30.4 0.2 fusion.46
  30.6 0.1 fusion.45
  30.7 0.1 fusion.44
  30.8 0.2 fusion.46
  31.0 0.1 fusion.45
  31.1 0.1 fusion.44
  31.2 0.2 fusion.46
  31.4 0.1 fusion.45
  31.6 0.2 fusion.46
  31.8 0.1 fusion.45
  32.0 0.2 fusion.46
  32.2 0.1 fusion.45
  32.4 0.2 fusion.46
  32.6 0.1 fusion.45
  32.7 0.1 fusion.44
  32.8 0.2 fusion.46
  33.0 0.1 reshape.24
  33.0 0.6 constant_dynamic-update-slice_fusion.15
  33.6 0.6 constant_dynamic-update-slice_fusion.14
  34.2 0.6 constant_dynamic-update-slice_fusion.13
  34.8 0.6 constant_dynamic-update-slice_fusion.12
  35.4 0.6 constant_dynamic-update-slice_fusion.11
  36.0 0.6 constant_dynamic-update-slice_fusion.10
  36.6 0.6 constant_dynamic-update-slice_fusion.9
  37.2 0.6 constant_dynamic-update-slice_fusion.8
  37.8 0.6 constant_dynamic-update-slice_fusion.7
  38.4 0.6 constant_dynamic-update-slice_fusion.6
  39.0 0.6 constant_dynamic-update-slice_fusion.5
  39.6 0.6 constant_dynamic-update-slice_fusion.4
  40.2 0.6 constant_dynamic-update-slice_fusion.3
  40.8 0.6 constant_dynamic-update-slice_fusion.2
  41.4 0.6 constant_dynamic-update-slice_fusion.1
  42.0 0.6 constant_dynamic-update-slice_fusion
  42.6 9.1 %all-to-all-start = ((f32[16,1,2,1152]{3,2,1,0:T(2,128)}), f32[16,1,2,1152]{3,2,1,0:T(2,128)S(1)}, u32[]{:S(2)}, u32[]{:S(2)}) async-start(f32[16,1,2,1152]{3,2,1,0:T(2,128)} %constant_dynamic-update-slice_fusion), calls=%async_computation | async-start | bytes 294912 | tf_op jit(solution)/shard_map/all_to_all | solution.py:45
  51.8 0.6 copy-done.5
  52.5 0.1 convert_reduce_fusion
  52.6 0.5 convolution_bitcast_fusion
  53.1 6.3 %all-to-all-done = f32[16,1,2,1152]{3,2,1,0:T(2,128)S(1)} async-done(((f32[16,1,2,1152]{3,2,1,0:T(2,128)}), f32[16,1,2,1152]{3,2,1,0:T(2,128)S(1)}, u32[]{:S(2)}, u32[]{:S(2)}) %all-to-all-start) | async-done | bytes 147488 | tf_op jit(solution)/shard_map/all_to_all | solution.py:45
  59.4 0.1 squeeze_reshape.3
  59.6 0.1 fusion.25
  59.7 0.8 copy-done.3
  60.5 0.9 convert_multiply_fusion
  61.3 1.3 dynamic-slice
  62.6 154.2 %all-reduce.4.cloned.1.call-done = f32[2,32,1152]{2,0,1:T(2,128)} async-done(((f32[2,32,1152]{2,0,1:T(2,128)}), f32[2,32,1152]{2,0,1:T(2,128)}) %all-reduce.4.cloned.1.call-update) | async-done | bytes 294928
  216.9 1.3 constant_dynamic-slice_fusion
  218.2 0.6 copy.26
  (38 shorter events, 0.8 us)
Async XLA Ops:
  6.5 46.0 %copy-start = (f32[16,5,32]{2,0,1:T(8,128)S(1)}, f32[16,5,32]{2,0,1:T(8,128)}, u32[]{:S(2)}) copy-start(f32[16,5,32]{2,0,1:T(8,128)} %param.12) | copy-start | bytes 30724
  6.5 0.7 copy-start.4
  7.2 0.9 copy-start.2
  18.5 10.4 %copy-start.1 = (f32[1,2,48,384]{3,2,1,0:T(8,128)S(1)}, f32[1,2,48,384]{3,2,1,0:T(8,128)}, u32[]{:S(2)}) copy-start(f32[1,2,48,384]{3,2,1,0:T(8,128)} %param.8) | copy-start | bytes 442372
  42.6 16.9 %all-to-all-start = ((f32[16,1,2,1152]{3,2,1,0:T(2,128)}), f32[16,1,2,1152]{3,2,1,0:T(2,128)S(1)}, u32[]{:S(2)}, u32[]{:S(2)}) async-start(f32[16,1,2,1152]{3,2,1,0:T(2,128)} %constant_dynamic-update-slice_fusion), calls=%async_computation | async-start | bytes 294912 | tf_op jit(solution)/shard_map/all_to_all | solution.py:45
  51.7 165.1 %all-reduce.4.cloned.1.call-start = ((), (), s32[]{:S(2)}) async-start(), calls=%async_computation.1 | async-start | bytes 589824
  51.8 0.7 copy-start.5
  59.5 0.9 copy-start.3
Sparse Core Ops, SparseCore 0:
  61.5 155.3 all-reduce.3
